TPU v7x, 512 devices: a whole 4x8x8 slice. The times are simulated.
512 devices in a mesh: col: 16 (over z, x_lo), sample: 32 (over x_hi, y, core).
Axes of the slice: x: 4 (x_hi: 2, x_lo: 2; x = x_hi * 2 + x_lo), y: 8, z: 8, core: 2. Of those that a mesh axis runs over, the one named last changes fastest.
Arguments:
- interaction: bfloat16 [2304, 8192], P('col', 'sample'), may hold values from -6 to 6
- out_grad: bfloat16 [8192, 4096], P('sample', 'col'), may hold values from -0.06591797 to 0.06591797
- top_weight: bfloat16 [2304, 4096], P(None, 'col'), may hold values from -0.125 to 0.125
- pooled: bfloat16 [48, 128, 8192], P(None, 'col', 'sample'), may hold values from -6 to 6
- bags: int32 [48, 4, 8192], P(None, None, 'sample'), may hold values from 0 to 511
- row_place: int32 [48, 512], replicated, may hold values from 0 to 511, each once within a row
Outputs:
- weight_grad: float32 [2304, 4096], P('sample', 'col')
- table_grad: float32 [128, 48, 512], P('col', None, 'sample')
Inputs may be any that keep to these rules, and one draw needn't show every extreme that they name: Each row of row_place holds every position 0 to 511 once.
All inputs are finite; a program needn't handle non-finite values.
Results may differ from a plain program's by a relative error of at most 0.0029.
Values may be sent and summed in bfloat16 or wider, within the bound.
A program may use at most 64 MiB of HBM per device.

v0:
```python
import jax
import jax.numpy as jnp
from jax import lax
from jax.sharding import PartitionSpec as P


def shards(interaction, out_grad, top_weight, pooled, bags, row_place):
    features = pooled.shape[0]
    samples = pooled.shape[2]
    weight_term = jnp.dot(
        lax.all_gather(interaction, "col", axis=0, tiled=True),
        out_grad,
        preferred_element_type=jnp.float32,
    )
    partial_value = lax.dot_general(
        top_weight, out_grad, (((1,), (1,)), ((), ())), preferred_element_type=jnp.float32
    )
    grad_cube = partial_value.reshape(features, features, samples)
    symmetric = grad_cube + jnp.transpose(grad_cube, (1, 0, 2))
    gram_grad = lax.psum(symmetric, "col").astype(jnp.bfloat16)
    pooled_grad = jnp.einsum("ijb,jeb->ieb", gram_grad, pooled, preferred_element_type=jnp.float32)
    rows_all = row_place.shape[1]
    row_ids = lax.broadcasted_iota(jnp.int32, (1, 1, rows_all), 2)

    def feature_rows(inputs):
        grad_feature, bag_feature, place_feature = inputs
        counts = jnp.sum((bag_feature[:, :, None] == row_ids).astype(jnp.float32), axis=0)
        by_row = jnp.dot(
            grad_feature,
            counts,
            precision=lax.Precision.HIGHEST,
            preferred_element_type=jnp.float32,
        )
        moving = (place_feature[:, None] == row_ids[0]).astype(jnp.float32)
        return jnp.dot(
            by_row, moving, precision=lax.Precision.HIGHEST, preferred_element_type=jnp.float32
        )

    dense_rows = lax.map(feature_rows, (pooled_grad, bags, row_place))
    dense_rows = jnp.transpose(dense_rows, (1, 0, 2))
    table_grad = lax.psum_scatter(dense_rows, "sample", scatter_dimension=2, tiled=True)
    weight_grad = lax.psum_scatter(weight_term, "sample", scatter_dimension=0, tiled=True)
    return (weight_grad, table_grad)


def solution(mesh):
    in_specs = (
        P("col", "sample"),
        P("sample", "col"),
        P(None, "col"),
        P(None, "col", "sample"),
        P(None, None, "sample"),
        P(),
    )
    out_specs = (P("sample", "col"), P("col", None, "sample"))
    return jax.shard_map(shards, mesh=mesh, in_specs=in_specs, out_specs=out_specs, check_vma=False)
```

profile of v0, /device:TPU:1, one launch (start us, length us, event | category | flops | bytes accessed | tf_op | source)
XLA Modules:
  0.0 711.2 jit_solution(6711608245679245035)
XLA Ops:
  9.3 1.4 fusion.16
  10.7 5.5 copy.13
  16.2 5.2 copy.14
  21.4 8.1 %bitcast_add_fusion = f32[48,48,256]{1,0,2:T(8,128)} fusion(f32[48,48,256]{1,0,2:T(8,128)} %copy.14, f32[48,48,256]{0,1,2:T(8,128)} %copy.13), kind=kLoop, calls=%fused_computation.14 | loop fusion | flops 589824 | bytes 7077888 | tf_op jit(solution)/shard_map/add | solution.py:19
  29.4 284.2 %all-reduce.1 = bf16[48,48,256]{1,0,2:T(8,128)(2,1)} all-reduce(f32[48,48,256]{1,0,2:T(8,128)} %bitcast_add_fusion), channel_id=1, replica_groups=mesh['col'=16,'sample'=32] {'col'}, use_global_device_ids=true, to_apply=%region_1.2 | all-reduce | flops 589824 | bytes 3538944 | tf_op jit(solution)/shard_map/psum | solution.py:20
  314.0 3.6 fusion.12
  318.1 122.3 %while.11 = (s32[]{:T(128)}, f32[48,8,512]{2,1,0:T(8,128)S(1)}, f32[48,8,256]{2,1,0:T(8,128)S(1)}, s32[48,4,256]{2,1,0:T(4,128)}, s32[48,512]{1,0:T(8,128)}, /*index=5*/s32[]{:T(128)}) while((s32[]{:T(128)}, f32[48,8,512]{2,1,0:T(8,128)S(1)}, f32[48,8,256]{2,1,0:T(8,128)S(1)}, s32[48,4,256]{2,1,0:T(4,128)}, s32[48,512]{1,0:T(8,128)}, ...), condition=%wide.region_4.5_spmd.clone, body=%wide.region_2.4_spmd.clone.sunk | while | flops 39452672 | bytes 1124437 | solution.py:39
  319.4 0.7 constant_dynamic-slice_fusion.2
  322.0 0.7 constant_dynamic-slice_fusion.2
  324.5 0.7 constant_dynamic-slice_fusion.2
  327.1 0.7 constant_dynamic-slice_fusion.2
  329.6 0.7 constant_dynamic-slice_fusion.2
  332.2 0.7 constant_dynamic-slice_fusion.2
  334.7 0.7 constant_dynamic-slice_fusion.2
  337.3 0.7 constant_dynamic-slice_fusion.2
  339.8 0.7 constant_dynamic-slice_fusion.2
  342.4 0.7 constant_dynamic-slice_fusion.2
  344.9 0.7 constant_dynamic-slice_fusion.2
  347.5 0.7 constant_dynamic-slice_fusion.2
  350.0 0.7 constant_dynamic-slice_fusion.2
  355.1 0.7 constant_dynamic-slice_fusion.2
  357.6 0.7 constant_dynamic-slice_fusion.2
  360.2 0.7 constant_dynamic-slice_fusion.2
  362.7 0.7 constant_dynamic-slice_fusion.2
  365.3 0.7 constant_dynamic-slice_fusion.2
  367.8 0.7 constant_dynamic-slice_fusion.2
  370.4 0.7 constant_dynamic-slice_fusion.2
  372.9 0.7 constant_dynamic-slice_fusion.2
  375.5 0.7 constant_dynamic-slice_fusion.2
  378.0 0.7 constant_dynamic-slice_fusion.2
  380.6 0.7 constant_dynamic-slice_fusion.2
  383.1 0.7 constant_dynamic-slice_fusion.2
  385.7 0.7 constant_dynamic-slice_fusion.2
  388.2 0.7 constant_dynamic-slice_fusion.2
  390.8 0.7 constant_dynamic-slice_fusion.2
  393.3 0.7 constant_dynamic-slice_fusion.2
  395.9 0.7 constant_dynamic-slice_fusion.2
  398.4 0.7 constant_dynamic-slice_fusion.2
  403.5 0.7 constant_dynamic-slice_fusion.2
  406.1 0.7 constant_dynamic-slice_fusion.2
  408.6 0.7 constant_dynamic-slice_fusion.2
  411.2 0.7 constant_dynamic-slice_fusion.2
  413.7 0.7 constant_dynamic-slice_fusion.2
  416.3 0.7 constant_dynamic-slice_fusion.2
  440.4 2.0 copy.17
  442.5 3.2 fusion.15
  445.7 125.3 %reduce-scatter.5.cloned.1.call-done = f32[8,48,16]{1,2,0:T(8,128)} async-done(((f32[8,48,512]{1,2,0:T(8,128)}), f32[8,48,16]{1,2,0:T(8,128)}) %reduce-scatter.5.cloned.1.call-update) | async-done | bytes 24592 | tf_op jit(solution)/shard_map/reduce_scatter | solution.py:41
  571.1 132.7 %reduce-scatter.3.cloned.1.call-done = f32[72,256]{1,0:T(8,128)} async-done(((f32[2304,256]{1,0:T(8,128)}), f32[72,256]{1,0:T(8,128)}) %reduce-scatter.3.cloned.1.call-update) | async-done | bytes 73744 | tf_op jit(solution)/shard_map/reduce_scatter | solution.py:42
  (219 shorter events, 96.9 us)
Async XLA Ops:
  8.0 1.3 copy-start
  8.0 434.5 %all-gather.2.cloned.1.call-start = ((), (), s32[]{:S(2)}) async-start(), calls=%async_computation.2 | async-start | bytes 1253376 | tf_op jit(solution)/shard_map/all_gather | solution.py:11
  8.7 562.3 %reduce-scatter.5.cloned.1.call-start = ((), (), s32[]{:S(2)}) async-start(), calls=%async_computation.4 | async-start | bytes 2162688 | tf_op jit(solution)/shard_map/reduce_scatter | solution.py:41
  29.4 284.2 %copy-start.2 = (bf16[48,8,256]{2,1,0:T(8,128)(2,1)S(1)}, bf16[48,8,256]{2,1,0:T(8,128)(2,1)}, u32[]{:S(2)}) copy-start(bf16[48,8,256]{2,1,0:T(8,128)(2,1)} %param.11) | copy-start | bytes 589828
  440.4 2.1 copy-start.1
  442.5 261.3 %reduce-scatter.3.cloned.1.call-start = ((), (), s32[]{:S(2)}) async-start(), calls=%async_computation.3 | async-start | bytes 2433024 | tf_op jit(solution)/shard_map/reduce_scatter | solution.py:42
Sparse Core Ops, SparseCore 0:
  11.1 95.0 all-gather.1
Sparse Core Ops, SparseCore 1:
  442.5 128.5 reduce-scatter.4
  577.0 126.7 reduce-scatter.2
where the time goes:
time: 722 us; the launch traced here: 711 us
  blocking collectives  284 us (39%)
  waiting for transfers between devices  259 us (36%)
  local copies, waits for them, and re-layouts  82.5 us (11%)
  matrix products  48.8 us (7%)
  other arithmetic  20.8 us (3%)
  between operations  15.5 us (2%)
    psum x1, blocking collectives, shards(): gram_grad = lax.psum(symmetric, 'col').astype(jnp.bfloat16)  284 us
    reduce_scatter x1, waiting for transfers between devices, shards(): lax.psum_scatter(weight_term, 'sample', scatter_dimension=0, tiled=True)  133 us
    reduce_scatter x1, waiting for transfers between devices, shards(): lax.psum_scatter(dense_rows, 'sample', scatter_dimension=2, tiled=True)  125 us
    dynamic_slice x48, local copies, waits for them, and re-layouts, shards(): dense_rows = lax.map(feature_rows, (pooled_grad, bags, row_place))  35.1 us
    eq x48, local copies, waits for them, and re-layouts, feature_rows(): bag_feature[:, :, None] == row_ids  33.4 us
    dot_general x48, matrix products, feature_rows(): jnp.dot(by_row, moving, precision=lax.Precision.HIGHEST, preferred_elemen...  23.4 us
    dot_general x48, matrix products, feature_rows(): jnp.dot(grad_feature, counts, precision=lax.Precision.HIGHEST, preferred_...  17.3 us
  transfers between devices with their start and end apart: 3, of which 2 were waited for; matrix products, arithmetic and copies ran while one was open for 21% of the time, Pallas kernels for 0%

commit v1 on v0

v1 whole, which is shorter than its diff:
```python
import jax
import jax.numpy as jnp
from jax import lax
from jax.experimental import pallas as pl
from jax.experimental.pallas import tpu as pltpu
from jax.sharding import PartitionSpec as P

MESH = pl.DeviceIdType.MESH
F32, BF16, I32 = jnp.float32, jnp.bfloat16, jnp.int32

F, E8, SB, HB, L, RT = 48, 8, 256, 256, 4, 512
NZ, NX, NY = 8, 2, 8
OFF = F // 2 + 1
CH = 80
WR = 72
IR = 144
GF = 16
NG = F // GF
EXT = F + F // 2
NT = (((1,), (1,)), ((), ()))


def swap_groups(v, rows, lanes):
    for k in (2, 1, 0):
        step = 1 << k
        up = (rows & step) == 0
        left = (lanes & (16 * step)) == 0
        a = pltpu.roll(pltpu.roll(v, 8 - step, 0), 16 * step, 1)
        b = a if k == 2 else pltpu.roll(pltpu.roll(v, step, 0), 128 - 16 * step, 1)
        v = jnp.where(up == left, v, jnp.where(up, a, b))
    return v


def kernel(
    inter, og, tw, pooled, bags, place,
    w_out, t_out,
    prod, sym, rs_buf, rx_buf, gg, cf, pf, pl_buf, iota_buf, cnt,
    ig, wt, wx, ws, wr, wf, wxh,
    td, tx, ts, tr, tf, txh,
    rs_s, rs_r, rx_s, rx_r, gg_s, gg_r, gp_s, gp_r, ig_s, ig_r, ip_s, ip_r,
    wx_s, wx_r, wy_s, wy_r, wh_s, wh_r, tx_s, tx_r, ty_s, ty_r, th_s, th_r,
    loc_s,
):
    col, smp = lax.axis_index("col"), lax.axis_index("sample")
    z, x = col // NX, col % NX
    xh, y, core = smp // 16, (smp // 2) % NY, smp % 2

    def col_dev(zz, xx):
        return {"col": zz * NX + xx, "sample": smp}

    def smp_dev(hh, yy, cc):
        return {"col": col, "sample": hh * 16 + yy * 2 + cc}

    zdev = [col_dev((z + 1) % NZ, x), col_dev((z + NZ - 1) % NZ, x)]
    xdev = col_dev(z, 1 - x)
    cdev = smp_dev(xh, y, 1 - core)
    hdev = smp_dev(1 - xh, y, core)

    def ydev(o):
        return smp_dev(xh, (y + o) % NY, core)

    def rc(src, dst, ss, rs, dev):
        return pltpu.make_async_remote_copy(
            src_ref=src, dst_ref=dst, send_sem=ss, recv_sem=rs, device_id=dev, device_id_type=MESH
        )

    barrier = pltpu.get_barrier_semaphore()
    friends = zdev + [xdev, cdev, hdev] + [ydev(o) for o in range(1, NY)]
    for dev in friends:
        pl.semaphore_signal(barrier, inc=1, device_id=dev, device_id_type=MESH)

    own = pltpu.make_async_copy(inter, ig.at[z, x], loc_s.at[0])
    own.start()

    for l in range(L):
        slot = bags[:, l, :]
        for h in range(2):
            ids = slot[:, h * 128:(h + 1) * 128]
            low, high = ids & 127, ids >> 7
            got = jnp.zeros((F, 128), I32)
            for k in range(4):
                part = jnp.take_along_axis(place[:, k * 128:(k + 1) * 128], low, axis=1, mode="promise_in_bounds")
                got = jnp.where(high == k, part, got)
            got = (got & 0xEF) | (((got >> 8) & 1) << 4) | (((got >> 4) & 1) << 8)
            pl_buf[l * F:(l + 1) * F, h * 128:(h + 1) * 128] = (got - 256).astype(F32)
    iota_buf[...] = (lax.broadcasted_iota(I32, (RT, SB), 0) - 256).astype(F32).astype(BF16)

    own.wait()
    pl.semaphore_wait(barrier, len(friends))

    class Gather:
        def __init__(self, buf, s, r, ps, pr):
            self.buf, self.s, self.r, self.ps, self.pr = buf, s, r, ps, pr

        def part(self, i):
            return x if i == 0 else 1 - x

        def copy(self, i, d, k):
            zz = (z + NZ - k) % NZ if d == 0 else (z + k) % NZ
            at = self.buf.at[zz, self.part(i)]
            return rc(at, at, self.s.at[i, d, k], self.r.at[i, d, k], zdev[d])

        def arrival(self, i, d, k):
            zz = (z + NZ - k - 1) % NZ if d == 0 else (z + k + 1) % NZ
            at = self.buf.at[zz, self.part(i)]
            return rc(at, at, self.s.at[i, d, k], self.r.at[i, d, k], zdev[d])

        def pair(self):
            at = self.buf.at[z, x]
            return rc(at, at, self.ps.at[0], self.pr.at[0], xdev)

        def has(self, i, d, k):
            return k < 3 or (k == 3 and i == d)

        def start0(self):
            for d in range(2):
                self.copy(0, d, 0).start()
            self.pair().start()

        def start1(self):
            at = self.buf.at[z, 1 - x]
            rc(at, at, self.ps.at[0], self.pr.at[0], xdev).wait_recv()
            for d in range(2):
                self.copy(1, d, 0).start()

        def hop(self, k):
            for i in range(2):
                for d in range(2):
                    if self.has(i, d, k - 1):
                        self.arrival(i, d, k - 1).wait_recv()
                    if self.has(i, d, k):
                        self.copy(i, d, k).start()

        def end(self):
            self.hop(4)

        def drain(self):
            self.pair().wait_send()
            for i in range(2):
                for d in range(2):
                    for k in range(4):
                        if self.has(i, d, k):
                            self.copy(i, d, k).wait_send()

    g_inter = Gather(ig, ig_s, ig_r, ip_s, ip_r)
    g_gram = Gather(gg, gg_s, gg_r, gp_s, gp_r)
    g_inter.start0()

    for b in range(6):
        r = lax.dot_general(tw[b * 384:(b + 1) * 384, :], og[...], NT, preferred_element_type=F32)
        for ii in range(8):
            i = b * 8 + ii
            blk = r[ii * F:(ii + 1) * F]
            for row in (i, i + F):
                if row < EXT:
                    for h in range(2):
                        half = blk[:, h * 128:(h + 1) * 128]
                        prod[h, row * EXT:row * EXT + F, :] = half
                        prod[h, row * EXT + F:(row + 1) * EXT, :] = half[:F // 2]
    for d in range(OFF):
        for h in range(2):
            both = prod[h, pl.ds(d, F, stride=EXT + 1), :] + prod[h, pl.ds(EXT * d, F, stride=EXT + 1), :]
            for m in range(3):
                at = d * F + 16 * m
                c, r0 = at // CH, at % CH
                sym[c // NX, c % NX, r0:r0 + 16, h * 128:(h + 1) * 128] = both[16 * m:16 * (m + 1)]
    sym[NZ - 1, NX - 1] = jnp.zeros((CH, SB), F32)

    def rs_copy(d, k):
        t = (z + 4 - k) % NZ if d == 0 else (z + 4 + k) % NZ
        if k == 0:
            return rc(sym.at[t, d], rs_buf.at[d, k, d], rs_s.at[d, k], rs_r.at[d, k], zdev[d])
        return rc(sym.at[t], rs_buf.at[d, k], rs_s.at[d, k], rs_r.at[d, k], zdev[d])

    def rs_step(k):
        for d in range(2):
            if k > 0:
                rs_copy(d, k - 1).wait_recv()
                t = (z + 4 - k) % NZ if d == 0 else (z + 4 + k) % NZ
                if k == 1:
                    sym[t, d] = sym[t, d] + rs_buf[d, 0, d]
                else:
                    sym[t] = sym[t] + rs_buf[d, k - 1]
            if k < 4:
                rs_copy(d, k).start()

    def count(f, carry):
        rows = [pl_buf[pl.ds(l * F + f, 1), :].astype(BF16) for l in range(L)]
        for ch in range(4):
            io = iota_buf[ch * 128:(ch + 1) * 128, :]
            acc = jnp.zeros((128, SB), BF16)
            for l in range(L):
                acc = acc + jnp.where(io == rows[l], jnp.ones((), BF16), jnp.zeros((), BF16))
            cnt[f, ch * 128:(ch + 1) * 128, :] = acc
        return carry

    def counts(lo, hi):
        lax.fori_loop(lo, hi, count, 0)

    rs_step(0)
    counts(0, 4)
    g_inter.start1()
    rs_step(1)
    counts(4, 12)
    rs_step(2)
    g_inter.hop(1)
    counts(12, 20)
    rs_step(3)
    g_inter.hop(2)
    counts(20, 28)
    rs_step(4)
    rxc = rc(sym.at[z, 1 - x], rx_buf, rx_s.at[0], rx_r.at[0], xdev)
    rxc.start()
    g_inter.hop(3)
    for j in range(F):
        v = pooled[j].astype(F32)
        pf[j] = v
        pf[j + F] = v
    rxc.wait_recv()
    gg[z, x] = (sym[z, x] + rx_buf[...]).astype(BF16)
    g_gram.start0()
    counts(28, 34)
    g_gram.start1()
    g_inter.end()
    g_gram.hop(1)

    def w_copy(cb):
        return rc(wt.at[cb, 1 - core], wx.at[cb], wx_s.at[cb], wx_r.at[cb], cdev)

    for zz in range(NZ):
        r = jnp.dot(ig[zz].reshape(2 * IR, SB), og[...], preferred_element_type=F32)
        for q in range(2):
            for cc in range(2):
                wt[zz * 2 + q, cc] = r[q * IR + cc * WR:q * IR + (cc + 1) * WR]
            w_copy(zz * 2 + q).start()
        if zz == 3:
            g_gram.hop(2)
    g_gram.hop(3)

    def wy_copy(o):
        return rc(ws.at[(y + o) % NY], wr.at[o], wy_s.at[o], wy_r.at[o], ydev(o))

    for o in range(NY):
        yy = (y + o) % NY
        for h in range(2):
            cb = h * NY + yy
            w_copy(cb).wait_recv()
            v = wt[cb, core] + wx[cb]
            ws[yy, h] = jnp.concatenate([v[:, :128], v[:, 128:]], axis=0).astype(BF16)
        if o > 0:
            wy_copy(o).start()
    counts(34, F)
    g_gram.end()

    for at in range(0, OFF * F, 16):
        c, r0 = at // CH, at % CH
        v = gg[c // NX, c % NX, r0:r0 + 16, :].astype(F32)
        d, i0 = at // F, at % F
        for base in (d * 2 * F + i0, d * 2 * F + F + i0):
            cf[base:base + 16, :] = v

    rows8 = lax.broadcasted_iota(I32, (8, 128), 0)
    lanes8 = lax.broadcasted_iota(I32, (8, 128), 1)

    def pooled_grad(i):
        accs = [jnp.zeros((E8, SB), F32) for _ in range(4)]
        n = 0
        for d in range(OFF):
            accs[n % 4] = accs[n % 4] + cf[pl.ds(i + d * 2 * F, 1), :] * pf[i + d]
            n += 1
        for d in range(1, OFF - 1):
            accs[n % 4] = accs[n % 4] + cf[pl.ds(i + (d * 2 * F + F - d), 1), :] * pf[i + (F - d)]
            n += 1
        v = (accs[0] + accs[1]) + (accs[2] + accs[3])
        hi = v.astype(BF16)
        lo = (v - hi.astype(F32)).astype(BF16)
        return jnp.concatenate([hi, lo], axis=0)

    def table_rows(f, fl, g, halves):
        r = lax.dot_general(halves, cnt[f], NT, preferred_element_type=F32)
        r = r[:E8] + r[E8:]
        for k in range(4):
            v = swap_groups(r[:, k * 128:(k + 1) * 128], rows8, lanes8)
            td[g, k // 2, pl.ds((k % 2) * 128 + fl, 8, stride=GF), :] = v

    def tx_copy(g):
        return rc(td.at[g, 1 - core], tx.at[g], tx_s.at[g], tx_r.at[g], cdev)

    def ty_copy(g, o):
        return rc(ts.at[g, (y + o) % NY], tr.at[g, o], ty_s.at[g, o], ty_r.at[g, o], ydev(o))

    def t_send(g):
        tx_copy(g).wait_recv()
        v = td[g, core] + tx[g]
        ts[g] = v.astype(BF16).reshape(NY, 2 * GF, 128)
        for o in range(1, NY):
            ty_copy(g, o).start()

    for g in range(NG):
        def body(fl, carry, g=g):
            table_rows(g * GF + fl, fl, g, pooled_grad(g * GF + fl))
            return carry

        lax.fori_loop(0, GF, body, 0)
        tx_copy(g).start()
        if g > 0:
            t_send(g - 1)
    t_send(NG - 1)

    wtot = ws[y].astype(F32)
    for o in range(1, NY):
        wy_copy(o).wait_recv()
        wtot = wtot + wr[o].astype(F32)
    wf[...] = wtot
    ws[y] = wtot.astype(BF16)
    whc = rc(ws.at[y, 1 - xh], wxh, wh_s.at[0], wh_r.at[0], hdev)
    whc.start()
    for g in range(NG):
        tot = ts[g, y].astype(F32)
        for o in range(1, NY):
            ty_copy(g, o).wait_recv()
            tot = tot + tr[g, o].astype(F32)
        tf[g] = tot.reshape(2, GF, 128)
    thc = rc(tf.at[:, 1 - xh], txh, th_s.at[0], th_r.at[0], hdev)
    thc.start()
    whc.wait_recv()
    tot = wf[xh] + wxh[...].astype(F32)
    w_out[:, :128] = tot[:WR]
    w_out[:, 128:] = tot[WR:]
    thc.wait_recv()
    for g in range(NG):
        tot = tf[g, xh] + txh[g]
        for e in range(E8):
            t_out[e, g * GF:(g + 1) * GF, :] = tot[:, e * 16:(e + 1) * 16]

    for d in range(2):
        for k in range(4):
            rs_copy(d, k).wait_send()
    rxc.wait_send()
    g_inter.drain()
    g_gram.drain()
    for cb in range(16):
        w_copy(cb).wait_send()
    for o in range(1, NY):
        wy_copy(o).wait_send()
    whc.wait_send()
    for g in range(NG):
        tx_copy(g).wait_send()
        for o in range(1, NY):
            ty_copy(g, o).wait_send()
    thc.wait_send()


def shards(interaction, out_grad, top_weight, pooled, bags, row_place):
    dma = pltpu.SemaphoreType.DMA
    v = pltpu.VMEM
    vmem = pl.BlockSpec(memory_space=pltpu.VMEM)
    gather_sems = [dma((2, 2, 4)), dma((2, 2, 4)), dma((1,)), dma((1,))]
    return pl.pallas_call(
        kernel,
        out_shape=(
            jax.ShapeDtypeStruct((WR, HB), F32),
            jax.ShapeDtypeStruct((E8, F, 16), F32),
        ),
        in_specs=[vmem] * 6,
        out_specs=(vmem, vmem),
        scratch_shapes=[
            v((2, EXT * EXT, 128), F32),
            v((NZ, NX, CH, SB), F32),
            v((2, 4, NX, CH, SB), F32),
            v((CH, SB), F32),
            v((NZ, NX, CH, SB), BF16),
            v((OFF * 2 * F, SB), F32),
            v((2 * F, E8, SB), F32),
            v((L * F, SB), F32),
            v((RT, SB), BF16),
            v((F, RT, SB), BF16),
            v((NZ, NX, IR, SB), BF16),
            v((16, 2, WR, HB), F32),
            v((16, WR, HB), F32),
            v((NY, 2, 2 * WR, 128), BF16),
            v((NY, 2, 2 * WR, 128), BF16),
            v((2, 2 * WR, 128), F32),
            v((2 * WR, 128), BF16),
            v((NG, 2, 16 * GF, 128), F32),
            v((NG, 16 * GF, 128), F32),
            v((NG, NY, 2 * GF, 128), BF16),
            v((NG, NY, 2 * GF, 128), BF16),
            v((NG, 2, GF, 128), F32),
            v((NG, GF, 128), F32),
            dma((2, 4)), dma((2, 4)), dma((1,)), dma((1,)),
            *gather_sems, *gather_sems,
            dma((16,)), dma((16,)), dma((NY,)), dma((NY,)), dma((1,)), dma((1,)),
            dma((NG,)), dma((NG,)), dma((NG, NY)), dma((NG, NY)), dma((1,)), dma((1,)),
            dma((1,)),
        ],
        compiler_params=pltpu.CompilerParams(
            collective_id=0, has_side_effects=True, vmem_limit_bytes=56 * 1024 * 1024
        ),
    )(interaction, out_grad, top_weight, pooled, bags, row_place)


def solution(mesh):
    in_specs = (
        P("col", "sample"),
        P("sample", "col"),
        P(None, "col"),
        P(None, "col", "sample"),
        P(None, None, "sample"),
        P(),
    )
    out_specs = (P("sample", "col"), P("col", None, "sample"))
    return jax.shard_map(shards, mesh=mesh, in_specs=in_specs, out_specs=out_specs, check_vma=False)
```

time: 722 us -> 95.4 us (0.13); the launches traced: 711 us -> 95.2 us
  blocking collectives: 284 us -> 0 us
  waiting for transfers between devices: 259 us -> 0 us
  Pallas kernels: 0 us -> 91.3 us
  local copies, waits for them, and re-layouts: 82.5 us -> 3.19 us
  matrix products: 48.8 us -> 0 us
  other arithmetic: 20.8 us -> 0 us
  between operations: 15.5 us -> 0.64 us
    psum x1 -> x0, blocking collectives: 284 us -> none  [shards(): gram_grad = lax.psum(symmetric, 'col').astype(jnp.bfloat16)]
    reduce_scatter x2 -> x0, waiting for transfers between devices: 258 us -> none  [the longest x1 133 us: shards(): lax.psum_scatter(weight_term, 'sample', scatter_dimension=0, tiled=True)]
    pallas_call x0 -> x1, Pallas kernels: none -> 91.3 us  [shards(): pl.pallas_call(kernel, out_shape=(jax.ShapeDtypeStruct((WR, HB), F32), ja...]
    dot_general x99 -> x0, matrix products: 48.8 us -> none  [the longest x48 23.4 us: feature_rows(): jnp.dot(by_row, moving, precision=lax.Precision.HIGHEST, preferred_elemen...]
    dynamic_slice x48 -> x0, local copies, waits for them, and re-layouts: 35.1 us -> none  [shards(): dense_rows = lax.map(feature_rows, (pooled_grad, bags, row_place))]
    eq x48 -> x0, local copies, waits for them, and re-layouts: 33.4 us -> none  [feature_rows(): bag_feature[:, :, None] == row_ids]
    reduce_sum x48 -> x0, other arithmetic: 12.7 us -> none  [feature_rows(): jnp.sum((bag_feature[:, :, None] == row_ids).astype(jnp.float32), axis=0)]
    reshape x2 -> x0, local copies, waits for them, and re-layouts: 10.7 us -> none  [shards(): grad_cube = partial_value.reshape(features, features, samples)]
  transfers between devices with their start and end apart: 3 -> 0, of which waited for: 2 -> 0; matrix products, arithmetic and copies ran while one was open for 21% -> 0% of each run, Pallas kernels for 0% -> 0%
where the time goes in v1:
time: 95.4 us; the launch traced here: 95.2 us
  Pallas kernels  91.3 us (96%)
  local copies, waits for them, and re-layouts  3.19 us (3%)
    pallas_call x1, Pallas kernels, shards(): pl.pallas_call(kernel, out_shape=(jax.ShapeDtypeStruct((WR, HB), F32), ja...  91.3 us

profile of v1, /device:TPU:1, one launch (start us, length us, event | category | flops | bytes accessed | tf_op | source)
XLA Modules:
  0.0 95.2 jit_solution(2816055417746257755)
XLA Ops:
  0.6 91.3 %shard_map.77 = (f32[72,256]{1,0:T(8,128)}, f32[8,48,16]{2,1,0:T(8,128)}) custom-call(bf16[144,256]{1,0:T(8,128)(2,1)} %inter.1, bf16[256,256]{1,0:T(8,128)(2,1)} %og.1, bf16[2304,256]{1,0:T(8,128)(2,1)} %tw.1, bf16[48,8,256]{2,1,0:T(8,128)(2,1)} %pooled.1, s32[48,4,256]{2,1,0:T(4,128)} %bags.1, s32[48,512]{1,0:T(8,128)} %place.1), custom_call_target="tpu_custom_call" | custom-call | tf_op jit(solution)/shard_map/pallas_call | solution.py:359
  92.0 1.7 %copy.8 = f32[8,48,16]{1,2,0:T(8,128)} copy(f32[8,48,16]{2,1,0:T(8,128)} %get-tuple-element.3) | data formatting | bytes 49152 | tf_op jit(solution)/shard_map/pallas_call | solution.py:359
  93.6 1.5 %copy.10 = f32[72,256]{1,0:T(8,128)} copy(f32[72,256]{1,0:T(8,128)} %get-tuple-element.6) | data formatting | bytes 147456

commit v2 on v1

v2 whole, which is shorter than its diff:
```python
import jax
import jax.numpy as jnp
from jax import lax
from jax.experimental import pallas as pl
from jax.experimental.pallas import tpu as pltpu
from jax.sharding import PartitionSpec as P

MESH = pl.DeviceIdType.MESH
F32, BF16, I32 = jnp.float32, jnp.bfloat16, jnp.int32

F, E8, SB, HB, L, RT = 48, 8, 256, 256, 4, 512
NZ, NX, NY = 8, 2, 8
OFF = F // 2 + 1
CH = 80
RA, RB = 32, 48
WR = 72
IR = 144
GF = 16
NG = F // GF
EXT = F + F // 2
NT = (((1,), (1,)), ((), ()))


def take(v, at, axis):
    return jnp.take_along_axis(v, at, axis=axis, mode="promise_in_bounds")


def kernel(
    inter_hbm, og_hbm, tw_hbm, pooled_hbm, bags_hbm, place_hbm,
    w_out, t_out,
    og, tw, pooled, bags, place,
    prod, sym, ra_buf, rb_buf, bx_buf, rx_buf, gg, cf, pf, pl_buf, iota_buf, cnt,
    ig, wt, wx, ws, wr, wf, wxh,
    td, tx, ts, tr, tf, txh,
    ra_s, ra_r, rb_s, rb_r, bx_s, bx_r, rx_s, rx_r,
    ga_s, ga_r, gx_s, gx_r, gb_s, gb_r, gp_s, gp_r,
    ia_s, ia_r, ix_s, ix_r, ib_s, ib_r, ip_s, ip_r,
    wx_s, wx_r, wy_s, wy_r, wh_s, wh_r, tx_s, tx_r, ty_s, ty_r, th_s, th_r,
    loc_s,
):
    col, smp = lax.axis_index("col"), lax.axis_index("sample")
    z, x = col // NX, col % NX
    xh, y, core = smp // 16, (smp // 2) % NY, smp % 2

    def col_dev(zz, xx):
        return {"col": zz * NX + xx, "sample": smp}

    def smp_dev(hh, yy, cc):
        return {"col": col, "sample": hh * 16 + yy * 2 + cc}

    zdev = [col_dev((z + 1) % NZ, x), col_dev((z + NZ - 1) % NZ, x)]
    xdev = col_dev(z, 1 - x)
    cdev = smp_dev(xh, y, 1 - core)
    hdev = smp_dev(1 - xh, y, core)

    def ydev(o):
        return smp_dev(xh, (y + o) % NY, core)

    sent = []

    class Copy:
        def __init__(self, src, dst, sems, at, dev):
            self.key = (id(sems[1]), at)
            self.copy = pltpu.make_async_remote_copy(
                src_ref=src, dst_ref=dst, send_sem=sems[0].at[at], recv_sem=sems[1].at[at],
                device_id=dev, device_id_type=MESH,
            )

        def start(self):
            self.copy.start()
            sent.append(self)

        def wait_recv(self):
            self.copy.wait_recv()

    def rc(src, dst, sems, at, dev):
        return Copy(src, dst, sems, at, dev)

    barrier = pltpu.get_barrier_semaphore()
    friends = zdev + [xdev, cdev, hdev] + [ydev(o) for o in range(1, NY)]
    for dev in friends:
        pl.semaphore_signal(barrier, inc=1, device_id=dev, device_id_type=MESH)

    loads = [
        pltpu.make_async_copy(src, dst, loc_s.at[n])
        for n, (src, dst) in enumerate(
            ((inter_hbm, ig.at[z, x]), (og_hbm, og), (tw_hbm, tw), (pooled_hbm, pooled), (bags_hbm, bags), (place_hbm, place))
        )
    ]
    for load in loads:
        load.start()
    loads[0].wait()
    pl.semaphore_wait(barrier, len(friends))

    def find_places():
        for l in range(L):
            slot = bags[:, l, :]
            for h in range(2):
                ids = slot[:, h * 128:(h + 1) * 128]
                low, high = ids & 127, ids >> 7
                got = jnp.zeros((F, 128), I32)
                for k in range(4):
                    part = take(place[:, k * 128:(k + 1) * 128], low, 1)
                    got = jnp.where(high == k, part, got)
                got = (got & 0xEF) | (((got >> 8) & 1) << 4) | (((got >> 4) & 1) << 8)
                pl_buf[l * F:(l + 1) * F, h * 128:(h + 1) * 128] = (got - 256).astype(F32)
        iota_buf[...] = (lax.broadcasted_iota(I32, (RT, SB), 0) - 256).astype(F32).astype(BF16)

    class Gather:
        def __init__(self, buf, cut, half, za, xa, zb, xb):
            self.buf, self.cut, self.half, self.rows = buf, cut, half, buf.shape[2]
            self.za, self.xa, self.zb, self.xb = za, xa, zb, xb

        def first(self, d, k, held):
            m = (NZ - k if d == 0 else k) if held else (NZ - k - 1 if d == 0 else k + 1)
            lo, hi = (0, self.cut) if k < 3 else ((0, self.half), (self.half, self.cut))[d]
            at = self.buf.at[(z + m) % NZ, x, pl.ds(lo, hi - lo)]
            return rc(at, at, self.za, (d, k), zdev[d])

        def across(self, m, xx):
            at = self.buf.at[(z + m) % NZ, xx, pl.ds(0, self.cut)]
            return rc(at, at, self.xa, (m % NZ,), xdev)

        def second(self, i, d, k, held):
            m = (NZ - k if d == 0 else k) if held else (NZ - k - 1 if d == 0 else k + 1)
            at = self.buf.at[(z + m) % NZ, x if i == 0 else 1 - x, pl.ds(self.cut, self.rows - self.cut)]
            return rc(at, at, self.zb, (i, d, k), zdev[d])

        def pair(self, xx):
            at = self.buf.at[z, xx, pl.ds(self.cut, self.rows - self.cut)]
            return rc(at, at, self.xb, (0,), xdev)

        def has(self, i, d, k):
            return k < 3 or (k == 3 and i == d)

        def start(self):
            self.pair(x).start()
            for d in range(2):
                self.first(d, 0, True).start()
            for d in range(2):
                self.second(0, d, 0, True).start()
            self.across(0, x).start()

        def start_pair(self):
            self.pair(1 - x).wait_recv()
            for d in range(2):
                self.second(1, d, 0, True).start()

        def hop_first(self, k):
            for d in range(2):
                self.first(d, k - 1, False).wait_recv()
                if k < 4:
                    self.first(d, k, True).start()
                    self.across(NZ - k if d == 0 else k, x).start()
            if k == 4:
                self.across(4, x).start()

        def hop_second(self, k):
            for i in range(2):
                for d in range(2):
                    if self.has(i, d, k - 1):
                        self.second(i, d, k - 1, False).wait_recv()
                    if self.has(i, d, k):
                        self.second(i, d, k, True).start()

        def end(self):
            for m in range(NZ):
                self.across(m, 1 - x).wait_recv()

    g_inter = Gather(ig, 80, 48, (ia_s, ia_r), (ix_s, ix_r), (ib_s, ib_r), (ip_s, ip_r))
    g_gram = Gather(gg, 48, 32, (ga_s, ga_r), (gx_s, gx_r), (gb_s, gb_r), (gp_s, gp_r))
    g_inter.start()
    loads[1].wait()
    loads[2].wait()

    for b in range(6):
        r = lax.dot_general(tw[b * 384:(b + 1) * 384, :], og[...], NT, preferred_element_type=F32)
        for ii in range(8):
            i = b * 8 + ii
            blk = r[ii * F:(ii + 1) * F]
            for row in (i, i + F):
                if row < EXT:
                    for h in range(2):
                        half = blk[:, h * 128:(h + 1) * 128]
                        prod[h, row * EXT:row * EXT + F, :] = half
                        prod[h, row * EXT + F:(row + 1) * EXT, :] = half[:F // 2]
    for d in range(OFF):
        for h in range(2):
            both = prod[h, pl.ds(d, F, stride=EXT + 1), :] + prod[h, pl.ds(EXT * d, F, stride=EXT + 1), :]
            for m in range(3):
                at = d * F + 16 * m
                c, r0 = at // CH, at % CH
                sym[c // NX, c % NX, r0:r0 + 16, h * 128:(h + 1) * 128] = both[16 * m:16 * (m + 1)]
    sym[NZ - 1, NX - 1] = jnp.zeros((CH, SB), F32)

    def dest(d, k):
        return (z + 4 - k) % NZ if d == 0 else (z + 4 + k) % NZ

    def ra_copy(d, k):
        if k == 0:
            return rc(sym.at[dest(d, k), d, pl.ds(0, RA)], ra_buf.at[d, k, d], (ra_s, ra_r), (d, k), zdev[d])
        return rc(sym.at[dest(d, k), :, pl.ds(0, RA)], ra_buf.at[d, k], (ra_s, ra_r), (d, k), zdev[d])

    def ra_step(k):
        for d in range(2):
            if k > 0:
                ra_copy(d, k - 1).wait_recv()
                t = dest(d, k)
                if k == 1:
                    sym[t, d, :RA, :] = sym[t, d, :RA, :] + ra_buf[d, 0, d]
                else:
                    sym[t, :, :RA, :] = sym[t, :, :RA, :] + ra_buf[d, k - 1]
            if k < 4:
                ra_copy(d, k).start()

    def ra_swap():
        return rc(sym.at[z, 1 - x, pl.ds(0, RA)], rx_buf, (rx_s, rx_r), (0,), xdev)

    def bx_copy(m):
        return rc(sym.at[(z + m) % NZ, 1 - x, pl.ds(RA, RB)], bx_buf.at[m], (bx_s, bx_r), (m,), xdev)

    def bx_add(m):
        bx_copy(m).wait_recv()
        t = (z + m) % NZ
        sym[t, x, RA:, :] = sym[t, x, RA:, :] + bx_buf[m]

    def rb_copy(d, k):
        if k == 0:
            part = pl.ds(d * (RB // 2), RB // 2)
            return rc(sym.at[dest(d, k), x, pl.ds(RA + d * (RB // 2), RB // 2)], rb_buf.at[d, k, part], (rb_s, rb_r), (d, k), zdev[d])
        return rc(sym.at[dest(d, k), x, pl.ds(RA, RB)], rb_buf.at[d, k], (rb_s, rb_r), (d, k), zdev[d])

    def rb_step(k):
        if k == 0:
            bx_add(4)
        elif k < 4:
            bx_add(4 - k)
            bx_add(4 + k)
        else:
            bx_add(0)
        for d in range(2):
            if k > 0:
                rb_copy(d, k - 1).wait_recv()
                t = dest(d, k)
                if k == 1:
                    lo = d * (RB // 2)
                    hi = lo + RB // 2
                    sym[t, x, RA + lo:RA + hi, :] = sym[t, x, RA + lo:RA + hi, :] + rb_buf[d, 0, lo:hi, :]
                else:
                    sym[t, x, RA:, :] = sym[t, x, RA:, :] + rb_buf[d, k - 1]
            if k < 4:
                rb_copy(d, k).start()

    def count(f, carry):
        rows = [pl_buf[pl.ds(l * F + f, 1), :].astype(BF16) for l in range(L)]
        for ch in range(4):
            io = iota_buf[ch * 128:(ch + 1) * 128, :]
            acc = jnp.zeros((128, SB), BF16)
            for l in range(L):
                acc = acc + jnp.where(io == rows[l], jnp.ones((), BF16), jnp.zeros((), BF16))
            cnt[f, ch * 128:(ch + 1) * 128, :] = acc
        return carry

    def counts(lo, hi):
        lax.fori_loop(lo, hi, count, 0)

    ra_step(0)
    for m in (4, 3, 5, 2, 6, 1, 7, 0):
        bx_copy(m).start()
    for n in (3, 4, 5):
        loads[n].wait()
    find_places()
    g_inter.start_pair()
    counts(0, 4)
    ra_step(1)
    g_inter.hop_first(1)
    g_inter.hop_second(1)
    counts(4, 10)
    ra_step(2)
    rb_step(0)
    g_inter.hop_first(2)
    g_inter.hop_second(2)
    counts(10, 16)
    ra_step(3)
    rb_step(1)
    g_inter.hop_first(3)
    g_inter.hop_second(3)
    counts(16, 22)
    ra_step(4)
    ra_swap().start()
    rb_step(2)
    g_inter.hop_first(4)
    g_inter.hop_second(4)
    for j in range(F):
        v = pooled[j].astype(F32)
        pf[j] = v
        pf[j + F] = v
    rb_step(3)
    counts(22, 28)
    rb_step(4)
    ra_swap().wait_recv()
    gg[z, x, :RA, :] = (sym[z, x, :RA, :] + rx_buf[...]).astype(BF16)
    gg[z, x, RA:, :] = sym[z, x, RA:, :].astype(BF16)
    g_gram.start()
    g_inter.end()

    def w_copy(cb):
        return rc(wt.at[cb, 1 - core], wx.at[cb], (wx_s, wx_r), (cb,), cdev)

    for zz in range(NZ):
        r = jnp.dot(ig[zz].reshape(2 * IR, SB), og[...], preferred_element_type=F32)
        for q in range(2):
            for cc in range(2):
                wt[zz * 2 + q, cc] = r[q * IR + cc * WR:q * IR + (cc + 1) * WR]
            w_copy(zz * 2 + q).start()
        if zz == 2:
            g_gram.start_pair()
        if zz == 5:
            g_gram.hop_first(1)
            g_gram.hop_second(1)
    g_gram.hop_first(2)
    g_gram.hop_second(2)

    def wy_copy(o):
        return rc(ws.at[(y + o) % NY], wr.at[o], (wy_s, wy_r), (o,), ydev(o))

    for o in range(NY):
        yy = (y + o) % NY
        for h in range(2):
            cb = h * NY + yy
            w_copy(cb).wait_recv()
            v = wt[cb, core] + wx[cb]
            ws[yy, h] = jnp.concatenate([v[:, :128], v[:, 128:]], axis=0).astype(BF16)
        if o > 0:
            wy_copy(o).start()
        if o == 3:
            g_gram.hop_first(3)
            g_gram.hop_second(3)
    counts(28, F)
    g_gram.hop_first(4)
    g_gram.hop_second(4)
    g_gram.end()

    for at in range(0, OFF * F, 16):
        c, r0 = at // CH, at % CH
        v = gg[c // NX, c % NX, r0:r0 + 16, :].astype(F32)
        d, i0 = at // F, at % F
        for base in (d * 2 * F + i0, d * 2 * F + F + i0):
            cf[base:base + 16, :] = v

    row = lax.broadcasted_iota(I32, (8, 128), 0)
    lane = lax.broadcasted_iota(I32, (8, 128), 1)
    grp, low4 = lane >> 4, lane & 15
    turn_a = (((grp + row) & 7) << 4) | low4
    turn_b = (row - grp) & 7
    turn_c = (((row - grp) & 7) << 4) | low4

    def pooled_grad(i):
        accs = [jnp.zeros((E8, SB), F32) for _ in range(4)]
        n = 0
        for d in range(OFF):
            accs[n % 4] = accs[n % 4] + cf[pl.ds(i + d * 2 * F, 1), :] * pf[i + d]
            n += 1
        for d in range(1, OFF - 1):
            accs[n % 4] = accs[n % 4] + cf[pl.ds(i + (d * 2 * F + F - d), 1), :] * pf[i + (F - d)]
            n += 1
        v = (accs[0] + accs[1]) + (accs[2] + accs[3])
        hi = v.astype(BF16)
        lo = (v - hi.astype(F32)).astype(BF16)
        return jnp.concatenate([hi, lo], axis=0)

    def table_rows(f, fl, g, halves):
        r = lax.dot_general(halves, cnt[f], NT, preferred_element_type=F32)
        r = r[:E8] + r[E8:]
        for k in range(4):
            v = take(take(take(r[:, k * 128:(k + 1) * 128], turn_a, 1), turn_b, 0), turn_c, 1)
            td[g, k // 2, pl.ds((k % 2) * 128 + fl, 8, stride=GF), :] = v

    def tx_copy(g):
        return rc(td.at[g, 1 - core], tx.at[g], (tx_s, tx_r), (g,), cdev)

    def ty_copy(g, o):
        return rc(ts.at[g, (y + o) % NY], tr.at[g, o], (ty_s, ty_r), (g, o), ydev(o))

    def t_send(g):
        tx_copy(g).wait_recv()
        v = td[g, core] + tx[g]
        ts[g] = v.astype(BF16).reshape(NY, 2 * GF, 128)
        for o in range(1, NY):
            ty_copy(g, o).start()

    halves = pooled_grad(0)
    for g in range(NG):
        def body(fl, halves, g=g):
            table_rows(g * GF + fl, fl, g, halves)
            return pooled_grad(g * GF + fl + 1)

        halves = lax.fori_loop(0, GF, body, halves, unroll=GF)
        tx_copy(g).start()
        if g > 0:
            t_send(g - 1)
    t_send(NG - 1)

    wtot = ws[y].astype(F32)
    for o in range(1, NY):
        wy_copy(o).wait_recv()
        wtot = wtot + wr[o].astype(F32)
    wf[...] = wtot
    ws[y] = wtot.astype(BF16)
    whc = rc(ws.at[y, 1 - xh], wxh, (wh_s, wh_r), (0,), hdev)
    whc.start()
    for g in range(NG):
        tot = ts[g, y].astype(F32)
        for o in range(1, NY):
            ty_copy(g, o).wait_recv()
            tot = tot + tr[g, o].astype(F32)
        tf[g] = tot.reshape(2, GF, 128)
    thc = rc(tf.at[:, 1 - xh], txh, (th_s, th_r), (0,), hdev)
    thc.start()
    whc.wait_recv()
    tot = wf[xh] + wxh[...].astype(F32)
    w_out[:, :128] = tot[:WR]
    w_out[:, 128:] = tot[WR:]
    thc.wait_recv()
    for g in range(NG):
        tot = tf[g, xh] + txh[g]
        for e in range(E8):
            t_out[e, g * GF:(g + 1) * GF, :] = tot[:, e * 16:(e + 1) * 16]

    for copy in sent:
        copy.copy.wait_send()


def shards(interaction, out_grad, top_weight, pooled, bags, row_place):
    dma = pltpu.SemaphoreType.DMA
    v = pltpu.VMEM
    vmem = pl.BlockSpec(memory_space=pltpu.VMEM)
    gather_sems = [dma(n) for n in ((2, 4), (NZ,), (2, 2, 4), (1,)) for _ in range(2)]
    return pl.pallas_call(
        kernel,
        out_shape=(
            jax.ShapeDtypeStruct((WR, HB), F32),
            jax.ShapeDtypeStruct((E8, F, 16), F32),
        ),
        in_specs=[pl.BlockSpec(memory_space=pl.ANY)] * 6,
        out_specs=(vmem, vmem),
        scratch_shapes=[
            v((SB, HB), BF16), v((F * F, HB), BF16), v((F, E8, SB), BF16), v((F, L, SB), I32), v((F, RT), I32),
            v((2, EXT * EXT, 128), F32),
            v((NZ, NX, CH, SB), F32),
            v((2, 4, NX, RA, SB), F32),
            v((2, 4, RB, SB), F32),
            v((NZ, RB, SB), F32),
            v((RA, SB), F32),
            v((NZ, NX, CH, SB), BF16),
            v((OFF * 2 * F, SB), F32),
            v((2 * F, E8, SB), F32),
            v((L * F, SB), F32),
            v((RT, SB), BF16),
            v((F, RT, SB), BF16),
            v((NZ, NX, IR, SB), BF16),
            v((16, 2, WR, HB), F32),
            v((16, WR, HB), F32),
            v((NY, 2, 2 * WR, 128), BF16),
            v((NY, 2, 2 * WR, 128), BF16),
            v((2, 2 * WR, 128), F32),
            v((2 * WR, 128), BF16),
            v((NG, 2, 16 * GF, 128), F32),
            v((NG, 16 * GF, 128), F32),
            v((NG, NY, 2 * GF, 128), BF16),
            v((NG, NY, 2 * GF, 128), BF16),
            v((NG, 2, GF, 128), F32),
            v((NG, GF, 128), F32),
            dma((2, 4)), dma((2, 4)), dma((2, 4)), dma((2, 4)), dma((NZ,)), dma((NZ,)), dma((1,)), dma((1,)),
            *gather_sems, *gather_sems,
            dma((16,)), dma((16,)), dma((NY,)), dma((NY,)), dma((1,)), dma((1,)),
            dma((NG,)), dma((NG,)), dma((NG, NY)), dma((NG, NY)), dma((1,)), dma((1,)),
            dma((6,)),
        ],
        compiler_params=pltpu.CompilerParams(
            collective_id=0, has_side_effects=True, vmem_limit_bytes=56 * 1024 * 1024
        ),
    )(interaction, out_grad, top_weight, pooled, bags, row_place)


def solution(mesh):
    in_specs = (
        P("col", "sample"),
        P("sample", "col"),
        P(None, "col"),
        P(None, "col", "sample"),
        P(None, None, "sample"),
        P(),
    )
    out_specs = (P("sample", "col"), P("col", None, "sample"))
    return jax.shard_map(shards, mesh=mesh, in_specs=in_specs, out_specs=out_specs, check_vma=False)
```

time: 95.4 us -> 78.8 us (0.83)
  Pallas kernels: 91.3 us -> 74.8 us
    pallas_call x1, Pallas kernels: 91.3 us -> 74.8 us  [shards(): pl.pallas_call(kernel, out_shape=(jax.ShapeDtypeStruct((WR, HB), F32), ja...]
where the time goes in v2:
time: 78.8 us; the launch traced here: 78.6 us
  Pallas kernels  74.8 us (95%)
  local copies, waits for them, and re-layouts  3.19 us (4%)
    pallas_call x1, Pallas kernels, shards(): pl.pallas_call(kernel, out_shape=(jax.ShapeDtypeStruct((WR, HB), F32), ja...  74.8 us
    pallas_call x1, local copies, waits for them, and re-layouts, shards(): pl.pallas_call(kernel, out_shape=(jax.ShapeDtypeStruct((WR, HB), F32), ja...  1.66 us

profile of v2, /device:TPU:1, one launch (start us, length us, event | category | flops | bytes accessed | tf_op | source)
XLA Modules:
  0.0 78.6 jit_solution(17070030755985053327)
XLA Ops:
  0.6 74.8 %shard_map.77 = (f32[72,256]{1,0:T(8,128)}, f32[8,48,16]{2,1,0:T(8,128)}) custom-call(bf16[144,256]{1,0:T(8,128)(2,1)} %inter_hbm.1, bf16[256,256]{1,0:T(8,128)(2,1)} %og_hbm.1, bf16[2304,256]{1,0:T(8,128)(2,1)} %tw_hbm.1, bf16[48,8,256]{2,1,0:T(8,128)(2,1)} %pooled_hbm.1, s32[48,4,256]{2,1,0:T(4,128)} %bags_hbm.1, s32[48,512]{1,0:T(8,128)} %place_hbm.1), custom_call_target="tpu_custom_call" | custom-call | tf_op jit(solution)/shard_map/pallas_call | solution.py:439
  75.4 1.7 %copy.8 = f32[8,48,16]{1,2,0:T(8,128)} copy(f32[8,48,16]{2,1,0:T(8,128)} %get-tuple-element.3) | data formatting | bytes 49152 | tf_op jit(solution)/shard_map/pallas_call | solution.py:439
  77.1 1.5 %copy.10 = f32[72,256]{1,0:T(8,128)} copy(f32[72,256]{1,0:T(8,128)} %get-tuple-element.6) | data formatting | bytes 147456

commit v3 on v2

--- a/solution.py
+++ b/solution.py
@@ -31,11 +31,11 @@
     og, tw, pooled, bags, place,
     prod, sym, ra_buf, rb_buf, bx_buf, rx_buf, gg, cf, pf, pl_buf, iota_buf, cnt,
     ig, wt, wx, ws, wr, wf, wxh,
-    td, tx, ts, tr, tf, txh,
+    td, tx, ts, tr,
     ra_s, ra_r, rb_s, rb_r, bx_s, bx_r, rx_s, rx_r,
     ga_s, ga_r, gx_s, gx_r, gb_s, gb_r, gp_s, gp_r,
     ia_s, ia_r, ix_s, ix_r, ib_s, ib_r, ip_s, ip_r,
-    wx_s, wx_r, wy_s, wy_r, wh_s, wh_r, tx_s, tx_r, ty_s, ty_r, th_s, th_r,
+    wx_s, wx_r, wy_s, wy_r, wh_s, wh_r, tx_s, tx_r, ty_s, ty_r,
     loc_s,
 ):
     col, smp = lax.axis_index("col"), lax.axis_index("sample")
@@ -49,12 +49,15 @@
         return {"col": col, "sample": hh * 16 + yy * 2 + cc}
 
     zdev = [col_dev((z + 1) % NZ, x), col_dev((z + NZ - 1) % NZ, x)]
+    zdev2 = [col_dev((z + 2) % NZ, x), col_dev((z + NZ - 2) % NZ, x)]
     xdev = col_dev(z, 1 - x)
     cdev = smp_dev(xh, y, 1 - core)
     hdev = smp_dev(1 - xh, y, core)
 
-    def ydev(o):
-        return smp_dev(xh, (y + o) % NY, core)
+    def ydev(o, h=0):
+        return smp_dev((xh + h) % 2, (y + o) % NY, core)
+
+    others = [(o, h) for o in range(NY) for h in range(2) if o + h > 0]
 
     sent = []
 
@@ -77,7 +80,7 @@
         return Copy(src, dst, sems, at, dev)
 
     barrier = pltpu.get_barrier_semaphore()
-    friends = zdev + [xdev, cdev, hdev] + [ydev(o) for o in range(1, NY)]
+    friends = zdev + zdev2 + [xdev, cdev] + [ydev(o, h) for o, h in others]
     for dev in friends:
         pl.semaphore_signal(barrier, inc=1, device_id=dev, device_id_type=MESH)
 
@@ -106,51 +109,65 @@
                 pl_buf[l * F:(l + 1) * F, h * 128:(h + 1) * 128] = (got - 256).astype(F32)
         iota_buf[...] = (lax.broadcasted_iota(I32, (RT, SB), 0) - 256).astype(F32).astype(BF16)
 
+    RING = ((0, 1), (1, 1), (2, 1), (3, 1))
+    RELAY = ((0, 1), (0, 2), (2, 1), (2, 2))
+
     class Gather:
-        def __init__(self, buf, cut, half, za, xa, zb, xb):
-            self.buf, self.cut, self.half, self.rows = buf, cut, half, buf.shape[2]
+        def __init__(self, buf, cut, half, hops, za, xa, zb, xb):
+            self.buf, self.cut, self.half, self.rows, self.hops = buf, cut, half, buf.shape[2], hops
             self.za, self.xa, self.zb, self.xb = za, xa, zb, xb
 
+        def block(self, d, k, held):
+            back = self.hops[k][0] if held else k + 1
+            dev = (zdev if self.hops[k][1] == 1 else zdev2)[d]
+            return (z + (NZ - back if d == 0 else back)) % NZ, dev
+
         def first(self, d, k, held):
-            m = (NZ - k if d == 0 else k) if held else (NZ - k - 1 if d == 0 else k + 1)
+            zz, dev = self.block(d, k, held)
             lo, hi = (0, self.cut) if k < 3 else ((0, self.half), (self.half, self.cut))[d]
-            at = self.buf.at[(z + m) % NZ, x, pl.ds(lo, hi - lo)]
-            return rc(at, at, self.za, (d, k), zdev[d])
+            at = self.buf.at[zz, x, pl.ds(lo, hi - lo)]
+            return rc(at, at, self.za, (d, k), dev)
 
         def across(self, m, xx):
             at = self.buf.at[(z + m) % NZ, xx, pl.ds(0, self.cut)]
             return rc(at, at, self.xa, (m % NZ,), xdev)
 
         def second(self, i, d, k, held):
-            m = (NZ - k if d == 0 else k) if held else (NZ - k - 1 if d == 0 else k + 1)
-            at = self.buf.at[(z + m) % NZ, x if i == 0 else 1 - x, pl.ds(self.cut, self.rows - self.cut)]
-            return rc(at, at, self.zb, (i, d, k), zdev[d])
+            zz, dev = self.block(d, k, held)
+            at = self.buf.at[zz, x if i == 0 else 1 - x, pl.ds(self.cut, self.rows - self.cut)]
+            return rc(at, at, self.zb, (i, d, k), dev)
 
         def pair(self, xx):
             at = self.buf.at[z, xx, pl.ds(self.cut, self.rows - self.cut)]
             return rc(at, at, self.xb, (0,), xdev)
 
-        def has(self, i, d, k):
-            return k < 3 or (k == 3 and i == d)
+        def after(self, k):
+            if self.hops is RING:
+                return (k,) if k < 4 else ()
+            return {0: (0, 1), 2: (2, 3)}.get(k, ())
 
         def start(self):
             self.pair(x).start()
-            for d in range(2):
-                self.first(d, 0, True).start()
-            for d in range(2):
-                self.second(0, d, 0, True).start()
+            for k in self.after(0):
+                for d in range(2):
+                    self.first(d, k, True).start()
+            for k in self.after(0):
+                for d in range(2):
+                    self.second(0, d, k, True).start()
             self.across(0, x).start()
 
         def start_pair(self):
             self.pair(1 - x).wait_recv()
-            for d in range(2):
-                self.second(1, d, 0, True).start()
+            for k in self.after(0):
+                for d in range(2):
+                    self.second(1, d, k, True).start()
 
         def hop_first(self, k):
             for d in range(2):
                 self.first(d, k - 1, False).wait_recv()
+                for n in self.after(k):
+                    self.first(d, n, True).start()
                 if k < 4:
-                    self.first(d, k, True).start()
                     self.across(NZ - k if d == 0 else k, x).start()
             if k == 4:
                 self.across(4, x).start()
@@ -158,17 +175,17 @@
         def hop_second(self, k):
             for i in range(2):
                 for d in range(2):
-                    if self.has(i, d, k - 1):
+                    if k < 4 or i == d:
                         self.second(i, d, k - 1, False).wait_recv()
-                    if self.has(i, d, k):
-                        self.second(i, d, k, True).start()
-
-        def end(self):
-            for m in range(NZ):
-                self.across(m, 1 - x).wait_recv()
-
-    g_inter = Gather(ig, 80, 48, (ia_s, ia_r), (ix_s, ix_r), (ib_s, ib_r), (ip_s, ip_r))
-    g_gram = Gather(gg, 48, 32, (ga_s, ga_r), (gx_s, gx_r), (gb_s, gb_r), (gp_s, gp_r))
+                    for n in self.after(k):
+                        if n < 3 or i == d:
+                            self.second(i, d, n, True).start()
+
+        def arrived(self, m):
+            self.across(m, 1 - x).wait_recv()
+
+    g_inter = Gather(ig, 80, 48, RING, (ia_s, ia_r), (ix_s, ix_r), (ib_s, ib_r), (ip_s, ip_r))
+    g_gram = Gather(gg, 48, 32, RELAY, (ga_s, ga_r), (gx_s, gx_r), (gb_s, gb_r), (gp_s, gp_r))
     g_inter.start()
     loads[1].wait()
     loads[2].wait()
@@ -264,82 +281,105 @@
     def counts(lo, hi):
         lax.fori_loop(lo, hi, count, 0)
 
+    def w_copy(cb):
+        return rc(wt.at[cb, 1 - core], wx.at[cb], (wx_s, wx_r), (cb,), cdev)
+
+    def w_mul(m):
+        g_inter.arrived(m)
+        zz = (z + m) % NZ
+        r = jnp.dot(ig[zz].reshape(2 * IR, SB), og[...], preferred_element_type=F32)
+        for q in range(2):
+            cb = zz * 2 + q
+            for cc in range(2):
+                wt[cb, cc] = r[q * IR + cc * WR:q * IR + (cc + 1) * WR]
+            w_copy(cb).start()
+
+    def wy_copy(o, h, dev):
+        return pltpu.make_async_remote_copy(
+            src_ref=ws.at[(y + o) % NY, h], dst_ref=wr.at[o, h], send_sem=wy_s.at[o, h], recv_sem=wy_r.at[o, h],
+            device_id=dev, device_id_type=MESH,
+        )
+
+    def w_add(m):
+        zz = (z + m) % NZ
+        for q in range(2):
+            cb = zz * 2 + q
+            w_copy(cb).wait_recv()
+            v = wt[cb, core] + wx[cb]
+            h, yy = cb // NY, cb % NY
+            ws[yy, h] = jnp.concatenate([v[:, :128], v[:, 128:]], axis=0).astype(BF16)
+            o = (yy + NY - y) % NY
+
+            @pl.when(o > 0)
+            def _():
+                wy_copy(o, h, smp_dev(xh, yy, core)).start()
+
     ra_step(0)
     for m in (4, 3, 5, 2, 6, 1, 7, 0):
         bx_copy(m).start()
     for n in (3, 4, 5):
         loads[n].wait()
     find_places()
+    counts(0, 6)
     g_inter.start_pair()
-    counts(0, 4)
+    counts(6, 14)
     ra_step(1)
+    rb_step(0)
     g_inter.hop_first(1)
     g_inter.hop_second(1)
-    counts(4, 10)
+    w_mul(0)
+    counts(14, 24)
     ra_step(2)
-    rb_step(0)
+    rb_step(1)
     g_inter.hop_first(2)
     g_inter.hop_second(2)
-    counts(10, 16)
+    w_add(0)
+    w_mul(1)
+    w_mul(7)
+    counts(24, 32)
     ra_step(3)
-    rb_step(1)
+    rb_step(2)
     g_inter.hop_first(3)
     g_inter.hop_second(3)
-    counts(16, 22)
+    w_add(1)
+    w_add(7)
+    w_mul(2)
+    w_mul(6)
+    counts(32, 40)
     ra_step(4)
     ra_swap().start()
-    rb_step(2)
+    rb_step(3)
     g_inter.hop_first(4)
     g_inter.hop_second(4)
-    for j in range(F):
-        v = pooled[j].astype(F32)
-        pf[j] = v
-        pf[j + F] = v
-    rb_step(3)
-    counts(22, 28)
+    w_add(2)
+    w_add(6)
+    w_mul(3)
+    w_mul(5)
+    counts(40, F)
     rb_step(4)
     ra_swap().wait_recv()
     gg[z, x, :RA, :] = (sym[z, x, :RA, :] + rx_buf[...]).astype(BF16)
     gg[z, x, RA:, :] = sym[z, x, RA:, :].astype(BF16)
     g_gram.start()
-    g_inter.end()
-
-    def w_copy(cb):
-        return rc(wt.at[cb, 1 - core], wx.at[cb], (wx_s, wx_r), (cb,), cdev)
-
-    for zz in range(NZ):
-        r = jnp.dot(ig[zz].reshape(2 * IR, SB), og[...], preferred_element_type=F32)
-        for q in range(2):
-            for cc in range(2):
-                wt[zz * 2 + q, cc] = r[q * IR + cc * WR:q * IR + (cc + 1) * WR]
-            w_copy(zz * 2 + q).start()
-        if zz == 2:
-            g_gram.start_pair()
-        if zz == 5:
-            g_gram.hop_first(1)
-            g_gram.hop_second(1)
+    w_mul(4)
+    w_add(3)
+    w_add(5)
+    g_gram.start_pair()
+    w_add(4)
+    for j in range(F):
+        v = pooled[j].astype(F32)
+        pf[j] = v
+        pf[j + F] = v
+    g_gram.hop_first(1)
     g_gram.hop_first(2)
+    g_gram.hop_second(1)
     g_gram.hop_second(2)
-
-    def wy_copy(o):
-        return rc(ws.at[(y + o) % NY], wr.at[o], (wy_s, wy_r), (o,), ydev(o))
-
-    for o in range(NY):
-        yy = (y + o) % NY
-        for h in range(2):
-            cb = h * NY + yy
-            w_copy(cb).wait_recv()
-            v = wt[cb, core] + wx[cb]
-            ws[yy, h] = jnp.concatenate([v[:, :128], v[:, 128:]], axis=0).astype(BF16)
-        if o > 0:
-            wy_copy(o).start()
-        if o == 3:
-            g_gram.hop_first(3)
-            g_gram.hop_second(3)
-    counts(28, F)
+    g_gram.hop_first(3)
     g_gram.hop_first(4)
+    g_gram.hop_second(3)
     g_gram.hop_second(4)
-    g_gram.end()
+    for m in range(NZ):
+        g_gram.arrived(m)
 
     for at in range(0, OFF * F, 16):
         c, r0 = at // CH, at % CH
@@ -379,15 +419,27 @@
     def tx_copy(g):
         return rc(td.at[g, 1 - core], tx.at[g], (tx_s, tx_r), (g,), cdev)
 
-    def ty_copy(g, o):
-        return rc(ts.at[g, (y + o) % NY], tr.at[g, o], (ty_s, ty_r), (g, o), ydev(o))
+    def ty_copy(g, o, h):
+        return rc(ts.at[g, (y + o) % NY, (xh + h) % 2], tr.at[g, o, h], (ty_s, ty_r), (g, o, h), ydev(o, h))
 
     def t_send(g):
         tx_copy(g).wait_recv()
         v = td[g, core] + tx[g]
-        ts[g] = v.astype(BF16).reshape(NY, 2 * GF, 128)
+        ts[g] = v.astype(BF16).reshape(NY, 2, GF, 128)
+        for o, h in others:
+            ty_copy(g, o, h).start()
+
+    def w_total():
+        wtot = ws[y].astype(F32)
         for o in range(1, NY):
-            ty_copy(g, o).start()
+            for h in range(2):
+                wy_copy(o, h, ydev(o)).wait_recv()
+            wtot = wtot + wr[o].astype(F32)
+        wf[...] = wtot
+        ws[y] = wtot.astype(BF16)
+        whc = rc(ws.at[y, 1 - xh], wxh, (wh_s, wh_r), (0,), hdev)
+        whc.start()
+        return whc
 
     halves = pooled_grad(0)
     for g in range(NG):
@@ -397,38 +449,33 @@
 
         halves = lax.fori_loop(0, GF, body, halves, unroll=GF)
         tx_copy(g).start()
+        if g == 0:
+            whc = w_total()
         if g > 0:
             t_send(g - 1)
     t_send(NG - 1)
 
-    wtot = ws[y].astype(F32)
-    for o in range(1, NY):
-        wy_copy(o).wait_recv()
-        wtot = wtot + wr[o].astype(F32)
-    wf[...] = wtot
-    ws[y] = wtot.astype(BF16)
-    whc = rc(ws.at[y, 1 - xh], wxh, (wh_s, wh_r), (0,), hdev)
-    whc.start()
     for g in range(NG):
-        tot = ts[g, y].astype(F32)
-        for o in range(1, NY):
-            ty_copy(g, o).wait_recv()
-            tot = tot + tr[g, o].astype(F32)
-        tf[g] = tot.reshape(2, GF, 128)
-    thc = rc(tf.at[:, 1 - xh], txh, (th_s, th_r), (0,), hdev)
-    thc.start()
+        tot = ts[g, y, xh].astype(F32)
+        for o, h in others:
+            ty_copy(g, o, h).wait_recv()
+            tot = tot + tr[g, o, h].astype(F32)
+        t_out[g * GF:(g + 1) * GF, :] = tot
     whc.wait_recv()
     tot = wf[xh] + wxh[...].astype(F32)
-    w_out[:, :128] = tot[:WR]
-    w_out[:, 128:] = tot[WR:]
-    thc.wait_recv()
-    for g in range(NG):
-        tot = tf[g, xh] + txh[g]
-        for e in range(E8):
-            t_out[e, g * GF:(g + 1) * GF, :] = tot[:, e * 16:(e + 1) * 16]
-
+    w_out[...] = tot
+
+    for o in range(1, NY):
+        for h in range(2):
+            wy_copy(o, h, ydev(o)).wait_send()
     for copy in sent:
         copy.copy.wait_send()
+
+
+def finish(w_sum, t_sum, w_out, t_out):
+    w_out[:, :128] = w_sum[:WR]
+    w_out[:, 128:] = w_sum[WR:]
+    t_out[...] = t_sum[...].T.reshape(E8, 16, F)
 
 
 def shards(interaction, out_grad, top_weight, pooled, bags, row_place):
@@ -436,11 +483,11 @@
     v = pltpu.VMEM
     vmem = pl.BlockSpec(memory_space=pltpu.VMEM)
     gather_sems = [dma(n) for n in ((2, 4), (NZ,), (2, 2, 4), (1,)) for _ in range(2)]
-    return pl.pallas_call(
+    outs = pl.pallas_call(
         kernel,
         out_shape=(
-            jax.ShapeDtypeStruct((WR, HB), F32),
-            jax.ShapeDtypeStruct((E8, F, 16), F32),
+            jax.ShapeDtypeStruct((2 * WR, 128), F32),
+            jax.ShapeDtypeStruct((F, 128), F32),
         ),
         in_specs=[pl.BlockSpec(memory_space=pl.ANY)] * 6,
         out_specs=(vmem, vmem),
@@ -467,20 +514,28 @@
             v((2 * WR, 128), BF16),
             v((NG, 2, 16 * GF, 128), F32),
             v((NG, 16 * GF, 128), F32),
-            v((NG, NY, 2 * GF, 128), BF16),
-            v((NG, NY, 2 * GF, 128), BF16),
-            v((NG, 2, GF, 128), F32),
-            v((NG, GF, 128), F32),
+            v((NG, NY, 2, GF, 128), BF16),
+            v((NG, NY, 2, GF, 128), BF16),
             dma((2, 4)), dma((2, 4)), dma((2, 4)), dma((2, 4)), dma((NZ,)), dma((NZ,)), dma((1,)), dma((1,)),
             *gather_sems, *gather_sems,
-            dma((16,)), dma((16,)), dma((NY,)), dma((NY,)), dma((1,)), dma((1,)),
-            dma((NG,)), dma((NG,)), dma((NG, NY)), dma((NG, NY)), dma((1,)), dma((1,)),
+            dma((16,)), dma((16,)), dma((NY, 2)), dma((NY, 2)), dma((1,)), dma((1,)),
+            dma((NG,)), dma((NG,)), dma((NG, NY, 2)), dma((NG, NY, 2)),
             dma((6,)),
         ],
         compiler_params=pltpu.CompilerParams(
             collective_id=0, has_side_effects=True, vmem_limit_bytes=56 * 1024 * 1024
         ),
     )(interaction, out_grad, top_weight, pooled, bags, row_place)
+    weights, tables = pl.pallas_call(
+        finish,
+        out_shape=(
+            jax.ShapeDtypeStruct((WR, HB), F32),
+            jax.ShapeDtypeStruct((E8, 16, F), F32),
+        ),
+        in_specs=[vmem, vmem],
+        out_specs=(vmem, vmem),
+    )(*outs)
+    return weights, jnp.transpose(tables, (0, 2, 1))
 
 
 def solution(mesh):

time: 78.8 us -> 68.4 us (0.87)
  Pallas kernels: 74.8 us -> 67.5 us
  local copies, waits for them, and re-layouts: 3.19 us -> 0 us
    pallas_call x1 -> x2, Pallas kernels: 74.8 us -> 67.5 us  [the longest x1 65.9 us: shards(): pl.pallas_call(kernel, out_shape=(jax.ShapeDtypeStruct((2 * WR, 128), F32...]
    pallas_call x1 -> x0, local copies, waits for them, and re-layouts: 1.66 us -> none  [shards(): pl.pallas_call(kernel, out_shape=(jax.ShapeDtypeStruct((WR, HB), F32), ja...]
    unnamed x1 -> x0, local copies, waits for them, and re-layouts: 1.52 us -> none
where the time goes in v3:
time: 68.4 us; the launch traced here: 68.2 us
  Pallas kernels  67.5 us (99%)
    pallas_call x1, Pallas kernels, shards(): pl.pallas_call(kernel, out_shape=(jax.ShapeDtypeStruct((2 * WR, 128), F32...  65.9 us
    pallas_call x1, Pallas kernels, shards(): pl.pallas_call(finish, out_shape=(jax.ShapeDtypeStruct((WR, HB), F32), ja...  1.62 us

profile of v3, /device:TPU:1, one launch (start us, length us, event | category | flops | bytes accessed | tf_op | source)
XLA Modules:
  0.0 68.2 jit_solution(7485746635937515981)
XLA Ops:
  0.6 65.9 %shard_map.77 = (f32[144,128]{1,0:T(8,128)}, f32[48,128]{1,0:T(8,128)}) custom-call(bf16[144,256]{1,0:T(8,128)(2,1)} %inter_hbm.1, bf16[256,256]{1,0:T(8,128)(2,1)} %og_hbm.1, bf16[2304,256]{1,0:T(8,128)(2,1)} %tw_hbm.1, bf16[48,8,256]{2,1,0:T(8,128)(2,1)} %pooled_hbm.1, s32[48,4,256]{2,1,0:T(4,128)} %bags_hbm.1, s32[48,512]{1,0:T(8,128)} %place_hbm.1), custom_call_target="tpu_custom_call" | custom-call | tf_op jit(solution)/shard_map/pallas_call | solution.py:486
  66.6 1.6 %shard_map.78 = (f32[72,256]{1,0:T(8,128)}, f32[8,16,48]{2,1,0:T(8,128)}) custom-call(f32[144,128]{1,0:T(8,128)} %get-tuple-element.6.w_sum, f32[48,128]{1,0:T(8,128)} %get-tuple-element.7.t_sum), custom_call_target="tpu_custom_call" | custom-call | tf_op jit(solution)/shard_map/pallas_call | solution.py:529

commit v4 on v3

--- a/solution.py
+++ b/solution.py
@@ -154,7 +154,6 @@
             for k in self.after(0):
                 for d in range(2):
                     self.second(0, d, k, True).start()
-            self.across(0, x).start()
 
         def start_pair(self):
             self.pair(1 - x).wait_recv()
@@ -315,8 +314,9 @@
                 wy_copy(o, h, smp_dev(xh, yy, core)).start()
 
     ra_step(0)
-    for m in (4, 3, 5, 2, 6, 1, 7, 0):
+    for m in (4, 3, 5):
         bx_copy(m).start()
+    g_inter.across(0, x).start()
     for n in (3, 4, 5):
         loads[n].wait()
     find_places()
@@ -325,12 +325,16 @@
     counts(6, 14)
     ra_step(1)
     rb_step(0)
+    bx_copy(2).start()
+    bx_copy(6).start()
     g_inter.hop_first(1)
     g_inter.hop_second(1)
     w_mul(0)
     counts(14, 24)
     ra_step(2)
     rb_step(1)
+    bx_copy(1).start()
+    bx_copy(7).start()
     g_inter.hop_first(2)
     g_inter.hop_second(2)
     w_add(0)
@@ -339,6 +343,7 @@
     counts(24, 32)
     ra_step(3)
     rb_step(2)
+    bx_copy(0).start()
     g_inter.hop_first(3)
     g_inter.hop_second(3)
     w_add(1)
@@ -361,6 +366,7 @@
     gg[z, x, :RA, :] = (sym[z, x, :RA, :] + rx_buf[...]).astype(BF16)
     gg[z, x, RA:, :] = sym[z, x, RA:, :].astype(BF16)
     g_gram.start()
+    g_gram.across(0, x).start()
     w_mul(4)
     w_add(3)
     w_add(5)
@@ -417,14 +423,14 @@
             td[g, k // 2, pl.ds((k % 2) * 128 + fl, 8, stride=GF), :] = v
 
     def tx_copy(g):
-        return rc(td.at[g, 1 - core], tx.at[g], (tx_s, tx_r), (g,), cdev)
+        return rc(td.at[g, 1 - core, pl.ds(0, 16 * GF)], tx.at[g], (tx_s, tx_r), (g,), cdev)
 
     def ty_copy(g, o, h):
         return rc(ts.at[g, (y + o) % NY, (xh + h) % 2], tr.at[g, o, h], (ty_s, ty_r), (g, o, h), ydev(o, h))
 
     def t_send(g):
         tx_copy(g).wait_recv()
-        v = td[g, core] + tx[g]
+        v = td[g, core, :16 * GF, :] + tx[g]
         ts[g] = v.astype(BF16).reshape(NY, 2, GF, 128)
         for o, h in others:
             ty_copy(g, o, h).start()
@@ -449,10 +455,9 @@
 
         halves = lax.fori_loop(0, GF, body, halves, unroll=GF)
         tx_copy(g).start()
-        if g == 0:
-            whc = w_total()
         if g > 0:
             t_send(g - 1)
+    whc = w_total()
     t_send(NG - 1)
 
     for g in range(NG):
@@ -493,7 +498,7 @@
         out_specs=(vmem, vmem),
         scratch_shapes=[
             v((SB, HB), BF16), v((F * F, HB), BF16), v((F, E8, SB), BF16), v((F, L, SB), I32), v((F, RT), I32),
-            v((2, EXT * EXT, 128), F32),
+            v((2, EXT * (EXT + 2), 128), F32),
             v((NZ, NX, CH, SB), F32),
             v((2, 4, NX, RA, SB), F32),
             v((2, 4, RB, SB), F32),
@@ -512,7 +517,7 @@
             v((NY, 2, 2 * WR, 128), BF16),
             v((2, 2 * WR, 128), F32),
             v((2 * WR, 128), BF16),
-            v((NG, 2, 16 * GF, 128), F32),
+            v((NG, 2, 17 * GF, 128), F32),
             v((NG, 16 * GF, 128), F32),
             v((NG, NY, 2, GF, 128), BF16),
             v((NG, NY, 2, GF, 128), BF16),

time: 68.4 us -> 65.9 us (0.963)
  Pallas kernels: 67.5 us -> 65.1 us
    pallas_call x1, Pallas kernels: 65.9 us -> 63.4 us  [shards(): pl.pallas_call(kernel, out_shape=(jax.ShapeDtypeStruct((2 * WR, 128), F32...]
where the time goes in v4:
time: 65.9 us; the launch traced here: 65.7 us
  Pallas kernels  65.1 us (99%)
    pallas_call x1, Pallas kernels, shards(): pl.pallas_call(kernel, out_shape=(jax.ShapeDtypeStruct((2 * WR, 128), F32...  63.4 us
    pallas_call x1, Pallas kernels, shards(): pl.pallas_call(finish, out_shape=(jax.ShapeDtypeStruct((WR, HB), F32), ja...  1.62 us

profile of v4, /device:TPU:1, one launch (start us, length us, event | category | flops | bytes accessed | tf_op | source)
XLA Modules:
  0.0 65.7 jit_solution(14694048252594258566)
XLA Ops:
  0.6 63.4 %shard_map.77 = (f32[144,128]{1,0:T(8,128)}, f32[48,128]{1,0:T(8,128)}) custom-call(bf16[144,256]{1,0:T(8,128)(2,1)} %inter_hbm.1, bf16[256,256]{1,0:T(8,128)(2,1)} %og_hbm.1, bf16[2304,256]{1,0:T(8,128)(2,1)} %tw_hbm.1, bf16[48,8,256]{2,1,0:T(8,128)(2,1)} %pooled_hbm.1, s32[48,4,256]{2,1,0:T(4,128)} %bags_hbm.1, s32[48,512]{1,0:T(8,128)} %place_hbm.1), custom_call_target="tpu_custom_call" | custom-call | tf_op jit(solution)/shard_map/pallas_call | solution.py:491
  64.1 1.6 %shard_map.78 = (f32[72,256]{1,0:T(8,128)}, f32[8,16,48]{2,1,0:T(8,128)}) custom-call(f32[144,128]{1,0:T(8,128)} %get-tuple-element.6.w_sum, f32[48,128]{1,0:T(8,128)} %get-tuple-element.7.t_sum), custom_call_target="tpu_custom_call" | custom-call | tf_op jit(solution)/shard_map/pallas_call | solution.py:534

commit v5 on v4

--- a/solution.py
+++ b/solution.py
@@ -81,7 +81,7 @@
 
     barrier = pltpu.get_barrier_semaphore()
     friends = zdev + zdev2 + [xdev, cdev] + [ydev(o, h) for o, h in others]
-    for dev in friends:
+    for dev in reversed(friends):
         pl.semaphore_signal(barrier, inc=1, device_id=dev, device_id_type=MESH)
 
     loads = [
@@ -271,9 +271,8 @@
         rows = [pl_buf[pl.ds(l * F + f, 1), :].astype(BF16) for l in range(L)]
         for ch in range(4):
             io = iota_buf[ch * 128:(ch + 1) * 128, :]
-            acc = jnp.zeros((128, SB), BF16)
-            for l in range(L):
-                acc = acc + jnp.where(io == rows[l], jnp.ones((), BF16), jnp.zeros((), BF16))
+            hits = [jnp.where(io == rows[l], jnp.ones((), BF16), jnp.zeros((), BF16)) for l in range(L)]
+            acc = (hits[0] + hits[1]) + (hits[2] + hits[3])
             cnt[f, ch * 128:(ch + 1) * 128, :] = acc
         return carry
 
@@ -321,8 +320,12 @@
         loads[n].wait()
     find_places()
     counts(0, 6)
+    for j in range(F):
+        v = pooled[j].astype(F32)
+        pf[j] = v
+        pf[j + F] = v
     g_inter.start_pair()
-    counts(6, 14)
+    counts(6, 10)
     ra_step(1)
     rb_step(0)
     bx_copy(2).start()
@@ -330,7 +333,7 @@
     g_inter.hop_first(1)
     g_inter.hop_second(1)
     w_mul(0)
-    counts(14, 24)
+    counts(10, 17)
     ra_step(2)
     rb_step(1)
     bx_copy(1).start()
@@ -340,7 +343,7 @@
     w_add(0)
     w_mul(1)
     w_mul(7)
-    counts(24, 32)
+    counts(17, 23)
     ra_step(3)
     rb_step(2)
     bx_copy(0).start()
@@ -350,7 +353,7 @@
     w_add(7)
     w_mul(2)
     w_mul(6)
-    counts(32, 40)
+    counts(23, 28)
     ra_step(4)
     ra_swap().start()
     rb_step(3)
@@ -360,7 +363,7 @@
     w_add(6)
     w_mul(3)
     w_mul(5)
-    counts(40, F)
+    counts(28, 34)
     rb_step(4)
     ra_swap().wait_recv()
     gg[z, x, :RA, :] = (sym[z, x, :RA, :] + rx_buf[...]).astype(BF16)
@@ -371,13 +374,11 @@
     w_add(3)
     w_add(5)
     g_gram.start_pair()
+    counts(34, 41)
     w_add(4)
-    for j in range(F):
-        v = pooled[j].astype(F32)
-        pf[j] = v
-        pf[j + F] = v
     g_gram.hop_first(1)
     g_gram.hop_first(2)
+    counts(41, F)
     g_gram.hop_second(1)
     g_gram.hop_second(2)
     g_gram.hop_first(3)
@@ -460,6 +461,12 @@
     whc = w_total()
     t_send(NG - 1)
 
+    for o in range(1, NY):
+        for h in range(2):
+            wy_copy(o, h, ydev(o)).wait_send()
+    for copy in sent:
+        copy.copy.wait_send()
+
     for g in range(NG):
         tot = ts[g, y, xh].astype(F32)
         for o, h in others:
@@ -469,12 +476,6 @@
     whc.wait_recv()
     tot = wf[xh] + wxh[...].astype(F32)
     w_out[...] = tot
-
-    for o in range(1, NY):
-        for h in range(2):
-            wy_copy(o, h, ydev(o)).wait_send()
-    for copy in sent:
-        copy.copy.wait_send()
 
 
 def finish(w_sum, t_sum, w_out, t_out):

time: 65.9 us -> 65.6 us (level)
  no operation moved by 1% of the time
where the time goes in v5:
time: 65.6 us; the launch traced here: 65.5 us
  Pallas kernels  64.8 us (99%)
    pallas_call x1, Pallas kernels, shards(): pl.pallas_call(kernel, out_shape=(jax.ShapeDtypeStruct((2 * WR, 128), F32...  63.2 us
    pallas_call x1, Pallas kernels, shards(): pl.pallas_call(finish, out_shape=(jax.ShapeDtypeStruct((WR, HB), F32), ja...  1.62 us

profile of v5, /device:TPU:1, one launch (start us, length us, event | category | flops | bytes accessed | tf_op | source)
XLA Modules:
  0.0 65.5 jit_solution(17491864231257136938)
XLA Ops:
  0.6 63.2 %shard_map.77 = (f32[144,128]{1,0:T(8,128)}, f32[48,128]{1,0:T(8,128)}) custom-call(bf16[144,256]{1,0:T(8,128)(2,1)} %inter_hbm.1, bf16[256,256]{1,0:T(8,128)(2,1)} %og_hbm.1, bf16[2304,256]{1,0:T(8,128)(2,1)} %tw_hbm.1, bf16[48,8,256]{2,1,0:T(8,128)(2,1)} %pooled_hbm.1, s32[48,4,256]{2,1,0:T(4,128)} %bags_hbm.1, s32[48,512]{1,0:T(8,128)} %place_hbm.1), custom_call_target="tpu_custom_call" | custom-call | tf_op jit(solution)/shard_map/pallas_call | solution.py:492
  63.9 1.6 %shard_map.78 = (f32[72,256]{1,0:T(8,128)}, f32[8,16,48]{2,1,0:T(8,128)}) custom-call(f32[144,128]{1,0:T(8,128)} %get-tuple-element.6.w_sum, f32[48,128]{1,0:T(8,128)} %get-tuple-element.7.t_sum), custom_call_target="tpu_custom_call" | custom-call | tf_op jit(solution)/shard_map/pallas_call | solution.py:535
